TPU v7x, 32 devices: a whole 2x2x4 slice. The times are simulated.
32 devices in a mesh: fsdp: 8 (over z, x), tp: 4 (over y, core).
Axes of the slice: x: 2, y: 2, z: 4, core: 2. Of those that a mesh axis runs over, the one named last changes fastest.
Arguments:
- gradients: bfloat16 [2, 2048, 8192], P(None, 'fsdp', 'tp'), may hold values from -120 to 120
- row_counts: int32 [8], replicated, may hold values from 128 to 256, as said below
- block_owner: int32 [2, 8], replicated, may hold values from 0 to 7, as said below
Outputs:
- update: bfloat16 [2, 2048, 8192], P(None, 'fsdp', 'tp')
- owned: bfloat16 [8192, 4096], P('fsdp', 'tp')
Inputs may be any that keep to these rules, and one draw needn't show every extreme that they name: `row_counts`: every count is a multiple of 128; some index holds exactly 256. `block_owner`: blocks whose columns lie on the same tp index have distinct owners.
All inputs are finite; a program needn't handle non-finite values.
Results may differ from a plain program's by a relative error of at most 0.005.
The roundings to bfloat16 on the way count: a program that leaves them out, or rounds other values in their place, can miss the bound.
Values may be sent and summed in bfloat16 or wider, within the bound.
A program may use at most 128 MiB of HBM per device.

v0:
```python
import jax
import jax.numpy as jnp
from jax import lax
from jax.sharding import PartitionSpec as P

BLOCK = 1024


damping = 0.01


def broadcast(block, axis, owner):
    block = jnp.where(lax.axis_index(axis) == owner, block, jnp.zeros_like(block))
    return lax.psum(block, axis)


def newton_root(statistic):
    identity = jnp.eye(statistic.shape[0], dtype=jnp.float32)
    scaling = 2.5 / jnp.sqrt(jnp.sum(statistic * statistic))
    scaled = scaling * statistic
    factor_one = (5.0 * identity - scaled) / 4.0
    square = jnp.dot(factor_one, factor_one, precision=lax.Precision.HIGHEST)
    inner_part = jnp.dot(square, scaled, precision=lax.Precision.HIGHEST)
    contracted = jnp.dot(square, inner_part, precision=lax.Precision.HIGHEST)
    factor_two = (5.0 * identity - contracted) / 4.0
    result = jnp.dot(
        jnp.sqrt(jnp.sqrt(scaling)) * factor_one, factor_two, precision=lax.Precision.HIGHEST
    )
    return result.astype(jnp.bfloat16)


def blank_root(statistic):
    return jnp.zeros(statistic.shape, jnp.bfloat16)


def unpack_pair(packed_sum, diagonal_sum):
    size = packed_sum.shape[-1]
    rows_idx = lax.broadcasted_iota(jnp.int32, (size, size), 0)
    cols_idx = lax.broadcasted_iota(jnp.int32, (size, size), 1)
    on_or_below = rows_idx >= cols_idx
    identity = jnp.eye(size, dtype=jnp.float32)
    below = jnp.where(rows_idx > cols_idx, packed_sum, 0.0)
    first_sum = jnp.where(on_or_below, packed_sum, 0.0) + jnp.swapaxes(below, -1, -2)
    above = jnp.where(on_or_below, 0.0, packed_sum)
    second_sum = above + jnp.swapaxes(above, -1, -2) + diagonal_sum[..., :, None] * identity
    return (first_sum, second_sum)


def unpack_all(packed_sum, diagonal_sum, block_total):
    first_sum, second_sum = unpack_pair(packed_sum, diagonal_sum)
    return jnp.stack([first_sum, second_sum], axis=1).reshape(block_total, BLOCK, BLOCK)


def body(gradients, row_counts, block_owner):
    fsdp_index = lax.axis_index("fsdp")
    tp_index = lax.axis_index("tp")
    layers, row_slots, columns = gradients.shape
    per_device = columns // BLOCK
    block_total = layers * per_device
    limit = row_counts[fsdp_index]
    valid_rows = (jnp.arange(row_slots, dtype=jnp.int32) < limit).astype(jnp.bfloat16)
    blocked = (gradients * valid_rows[None, :, None]).reshape(layers, row_slots, per_device, BLOCK)
    partial_value = jnp.einsum(
        "lrkb,lrke->lkbe", blocked, blocked, preferred_element_type=jnp.float32
    )
    partial_value = partial_value.reshape(block_total, BLOCK, BLOCK)
    identity = jnp.eye(BLOCK, dtype=jnp.float32)
    total_rows = jnp.sum(row_counts).astype(jnp.float32)
    local_owner = lax.dynamic_slice(
        block_owner, (jnp.int32(0), tp_index * per_device), (layers, per_device)
    )
    local_owner = local_owner.reshape(block_total)
    owned_mask = local_owner == fsdp_index
    rows_idx = lax.broadcasted_iota(jnp.int32, (BLOCK, BLOCK), 0)
    cols_idx = lax.broadcasted_iota(jnp.int32, (BLOCK, BLOCK), 1)
    on_or_below = rows_idx >= cols_idx
    first_src = partial_value[0::2]
    second_src = partial_value[1::2]
    packed = jnp.where(on_or_below, first_src, second_src)
    diagonal = jnp.diagonal(second_src, axis1=1, axis2=2)
    packed_sum, diagonal_sum = lax.psum((packed, diagonal), "fsdp")
    summed = unpack_all(packed_sum, diagonal_sum, block_total)
    statistic = summed / total_rows + damping * identity
    chosen = jnp.sum(jnp.where(owned_mask[:, None, None], statistic, 0.0), axis=0)
    owned_root = lax.cond(jnp.any(owned_mask), newton_root, blank_root, chosen)
    received = []
    for position in range(block_total):
        received.append(broadcast(owned_root, "fsdp", local_owner[position]))
    root_list = jnp.stack(received).reshape(layers, per_device, BLOCK, BLOCK)
    update = jnp.einsum("lrkb,lkbe->lrke", blocked, root_list, preferred_element_type=jnp.float32)
    return (update.astype(jnp.bfloat16).reshape(layers, row_slots, columns), owned_root)


def solution(mesh):
    placed = (P(None, "fsdp", "tp"), P(), P())
    return jax.shard_map(
        body,
        mesh=mesh,
        in_specs=placed,
        out_specs=(P(None, "fsdp", "tp"), P("fsdp", "tp")),
        check_vma=False,
    )
```

profile of v0, /device:TPU:0, one launch (start us, length us, event | category | flops | bytes accessed | tf_op | source)
XLA Modules:
  0.0 823.3 jit_solution(13109031683089435349)
XLA Ops:
  7.2 0.0 all-reduce.4.cloned.1.call-start
  7.2 0.3 iota_compare_fusion.4
  7.5 1.2 dynamic_slice.7
  8.8 0.6 compare_convert_fusion
  9.4 1.8 broadcast_multiply_fusion
  11.2 2.4 fusion.38
  13.7 6.6 fusion.45
  20.2 1.9 copy.55
  22.2 28.9 %fusion.46 = (f32[2,1024,1024]{2,0,1:T(2,128)}, f32[2,1024,1024]{2,0,1:T(2,128)}) fusion(f32[2,1024,1024]{2,1,0:T(8,128)} %get-tuple-element.90, f32[2,1024,1024]{2,1,0:T(8,128)} %get-tuple-element.91, pred[1024,1024]{1,0:T(8,128)(4,1)S(1)} %copy.55), kind=kLoop, calls=%fused_computation.66 | loop fusion | flops 2097152 | bytes 34603008
  51.1 0.0 all-reduce.4.cloned.1.call-update
  51.2 0.0 all-reduce.6.cloned.1.call-start
  51.2 0.6 copy-done.8
  51.8 0.7 reduce_sum.33
  52.5 0.7 compare_reduce_fusion
  54.5 12.5 %gather_fusion = f32[1024,2]{0,1:T(2,128)S(1)} fusion(f32[2,1024,1024]{2,0,1:T(2,128)} %get-tuple-element.92, s32[1024]{0:T(1024)S(1)} %bitcast.49), kind=kCustom, calls=%fused_computation | custom fusion | bytes 24576 | tf_op jit(solution)/shard_map/jit(diagonal)/gather | solution.py:80
  67.1 25.1 %psum.43 = f32[2,1024]{1,0:T(2,128)S(1)} all-reduce(f32[2,1024]{1,0:T(2,128)S(1)} %bitcast.55), channel_id=1, replica_groups=mesh['fsdp'=8,'tp'=4] {'fsdp'}, use_global_device_ids=true, to_apply=%region_2.3 | all-reduce | flops 2048 | bytes 16384 | tf_op jit(solution)/shard_map/psum | solution.py:81
  92.1 1.0 copy.48
  93.2 0.1 reshape.46
  93.2 0.7 fusion.47
  96.4 0.3 iota_compare_fusion.3
  96.7 2.4 fusion.35
  99.2 225.9 %all-reduce.4.cloned.1.call-done = f32[2,1024,1024]{2,0,1:T(2,128)} async-done(((f32[2,1024,1024]{2,0,1:T(2,128)}), f32[2,1024,1024]{2,0,1:T(2,128)}) %all-reduce.4.cloned.1.call-update) | async-done | bytes 8388624 | tf_op jit(solution)/shard_map/psum | solution.py:81
  325.1 11.0 %broadcast_select_fusion = f32[2,1024,1024]{2,0,1:T(2,128)} fusion(f32[2,1024,1024]{2,0,1:T(2,128)} %all-reduce.4.cloned.1.call-done, pred[1024,1024]{1,0:T(8,128)(4,1)S(1)} %copy.55), kind=kLoop, calls=%fused_computation.43 | loop fusion | flops 2097152 | bytes 17825792 | tf_op jit(solution)/shard_map/jit(_where)/select_n | solution.py:44
  336.0 17.1 %copy.47 = f32[2,1024,1024]{1,0,2:T(2,128)} copy(f32[2,1024,1024]{2,0,1:T(2,128)} %broadcast_select_fusion) | data formatting | bytes 16777216 | tf_op jit(solution)/shard_map/jit(_where)/select_n | solution.py:44
  353.1 17.1 %copy.42 = f32[2,1024,1024]{1,0,2:T(2,128)} copy(f32[2,1024,1024]{2,0,1:T(2,128)} %all-reduce.4.cloned.1.call-done) | data formatting | bytes 16777216 | tf_op jit(solution)/shard_map/psum | solution.py:81
  370.2 11.0 %broadcast_select_fusion.1 = f32[2,1024,1024]{1,0,2:T(2,128)} fusion(f32[2,1024,1024]{1,0,2:T(2,128)} %copy.42, pred[1024,1024]{0,1:T(8,128)(4,1)S(1)} %iota_compare_fusion.4), kind=kLoop, calls=%fused_computation.44 | loop fusion | flops 2097152 | bytes 17825792 | tf_op jit(solution)/shard_map/jit(_where)/select_n | solution.py:43
  381.2 17.2 %copy.44 = f32[2,1024,1024]{2,0,1:T(2,128)} copy(f32[2,1024,1024]{1,0,2:T(2,128)} %broadcast_select_fusion.1) | data formatting | bytes 16777216 | tf_op jit(solution)/shard_map/jit(_where)/select_n | solution.py:43
  398.3 11.3 %fusion.34 = f32[2,1,1024,1024]{3,0,2,1:T(2,128)S(1)} fusion(f32[2,1024,1024]{2,0,1:T(2,128)} %copy.44, f32[2,1024,1024]{1,0,2:T(2,128)} %copy.42, pred[1024,1024]{0,1:T(8,128)(4,1)S(1)} %iota_compare_fusion.3), kind=kLoop, calls=%fused_computation.42 | loop fusion | flops 4194304 | bytes 26214400 | tf_op jit(solution)/shard_map/stack | solution.py:51
  409.7 12.4 %fusion.33 = f32[2,1,1024,1024]{3,0,2,1:T(2,128)S(1)} fusion(f32[2,1024,1024]{1,0,2:T(2,128)} %copy.47, f32[1024,1024]{1,0:T(8,128)S(1)} %copy-done.2, f32[2,1024]{0,1:T(8,128)S(1)} %copy-done.6, f32[2,1024,1024]{2,0,1:T(2,128)} %all-reduce.4.cloned.1.call-done, pred[1024,1024]{1,0:T(8,128)(4,1)S(1)} %copy.55), kind=kLoop, calls=%fused_computation.40 | loop fusion | flops 8388608 | bytes 30416896 | tf_op jit(solution)/shard_map/stack | solution.py:51
  422.1 8.6 %pad_maximum_fusion = f32[2,2,1024,1024]{3,0,2,1:T(2,128)} fusion(f32[2,1,1024,1024]{3,0,2,1:T(2,128)S(1)} %fusion.33, f32[2,1,1024,1024]{3,0,2,1:T(2,128)S(1)} %fusion.34), kind=kLoop, calls=%fused_computation.35 | loop fusion | flops 4194304 | bytes 33554432 | tf_op jit(solution)/shard_map/stack | solution.py:51
  430.7 2.2 iota.86
  432.9 2.5 iota.87
  435.4 89.7 %conditional.1 = (bf16[1024,1024]{1,0:T(8,128)(2,1)S(1)}) conditional(s32[]{:T(128)} %convert_element_type.32, () %tuple.18, (s32[]{:T(128)}, s32[2,2]{1,0:T(2,128)S(1)}, f32[]{:T(128)}, f32[2,2,1024,1024]{3,0,2,1:T(2,128)}, s32[1,1024,1024]{2,1,0:T(8,128)}, /*index=5*/s32[1,1024,1024]{2,1,0:T(8,128)}) %tuple.19), branch_computations={%region_4.5_spmd, %region_5.8_spmd} | conditional | flops 51576307712 | bytes 119537840 | solution.py:85
  435.8 4.4 select_bitcast_fusion
  440.2 13.6 %fusion.2 = f32[1024,1024]{1,0:T(8,128)S(1)} fusion(f32[2,2,1024,1024]{3,0,2,1:T(2,128)} %get-tuple-element.79, f32[1024,1024]{1,0:T(8,128)S(1)} %select_bitcast_fusion, f32[]{:T(128)} %get-tuple-element.55, pred[2,2]{1,0:T(4,128)(4,1)S(1)} %broadcast_compare_fusion), kind=kLoop, calls=%fused_computation.4 | loop fusion | flops 15728640 | bytes 25165832 | tf_op jit(solution)/shard_map/reduce_sum | solution.py:84
  453.8 1.9 copy-done
  455.8 1.7 multiply_reduce_fusion
  458.1 19.4 %fusion.6 = f32[1024,1024]{1,0:T(8,128)S(1)} fusion(f32[1024,1024]{1,0:T(8,128)} %copy-done, f32[]{:T(128)S(6)} %div.15), kind=kOutput, calls=%fused_computation.9 | convolution fusion | flops 12890144768 | bytes 8388612 | tf_op jit(solution)/shard_map/cond/branch_1_fun/dot_general | solution.py:22
  477.5 13.4 %fusion.9 = f32[1024,1024]{1,0:T(8,128)S(1)} fusion(f32[1024,1024]{1,0:T(8,128)S(1)} %fusion.6, f32[1024,1024]{1,0:T(8,128)S(1)} %copy-done.1, f32[]{:T(128)S(6)} %div.15), kind=kOutput, calls=%fused_computation.15 | convolution fusion | flops 12885950464 | bytes 12582916 | tf_op jit(solution)/shard_map/cond/branch_1_fun/dot_general | solution.py:23
  491.0 15.0 %fusion.48 = f32[1024,1024]{1,0:T(8,128)} fusion(f32[1024,1024]{1,0:T(8,128)S(1)} %fusion.6, f32[1024,1024]{1,0:T(8,128)S(1)} %fusion.9), kind=kOutput, calls=%fused_computation.68 | convolution fusion | flops 12884901888 | bytes 12582912 | tf_op jit(solution)/shard_map/cond/branch_1_fun/dot_general | solution.py:24
  506.0 18.7 %fusion.21 = bf16[1024,1024]{1,0:T(8,128)(2,1)S(1)} fusion(f32[1024,1024]{1,0:T(8,128)} %fusion.48, f32[1024,1024]{1,0:T(8,128)} %copy-done, f32[]{:T(128)S(6)} %mul.47, f32[]{:T(128)S(6)} %div.15), kind=kOutput, calls=%fused_computation.27 | convolution fusion | flops 12895387648 | bytes 10485768 | tf_op jit(solution)/shard_map/cond/branch_1_fun/dot_general | solution.py:26
  525.0 3.5 select_bitcast_fusion.4
  528.6 0.4 copy-done.5
  528.9 0.0 all-reduce.6.cloned.1.call-update
  529.0 270.9 %all-reduce.6.cloned.1.call-done = (bf16[1,1024,1024]{2,1,0:T(8,128)(2,1)}, bf16[1,1024,1024]{2,1,0:T(8,128)(2,1)}, bf16[1,1024,1024]{2,1,0:T(8,128)(2,1)}, bf16[1,1024,1024]{2,1,0:T(8,128)(2,1)}) async-done(((bf16[1,1024,1024]{2,1,0:T(8,128)(2,1)}, bf16[1,1024,1024]{2,1,0:T(8,128)(2,1)}, bf16[1,1024,1024]{2,1,0:T(8,128)(2,1)}, bf16[1,1024,1024]{2,1,0:T(8,128)(2,1)}), (bf16[1,1024,1024]{2,1,0:T(8,128)(2,1)}, ...) | async-done | bytes 8388624 | tf_op jit(solution)/shard_map/psum | solution.py:14
  799.8 7.3 pad_maximum_fusion.1
  807.1 6.4 fusion.40
  813.6 2.4 copy.52
  (17 shorter events, 0.0 us)
Async XLA Ops:
  7.2 317.9 %all-reduce.4.cloned.1.call-start = ((), (), s32[]{:S(2)}) async-start(), calls=%async_computation | async-start | bytes 16777216 | tf_op jit(solution)/shard_map/psum | solution.py:81
  11.2 2.4 copy-start.3
  51.1 0.7 copy-start.8
  51.1 1.4 copy-start.7
  51.2 748.7 %all-reduce.6.cloned.1.call-start = ((), (), s32[]{:S(2)}) async-start(), calls=%async_computation.1 | async-start | bytes 16777216 | tf_op jit(solution)/shard_map/psum | solution.py:14
  398.3 11.3 %copy-start.2 = (f32[1024,1024]{1,0:T(8,128)S(1)}, f32[1024,1024]{1,0:T(8,128)}, u32[]{:S(2)}) copy-start(f32[1024,1024]{1,0:T(8,128)} %fusion.35) | copy-start | bytes 12582916
  398.3 11.3 %copy-start.6 = (f32[2,1024]{0,1:T(8,128)S(1)}, f32[2,1024]{0,1:T(8,128)}, u32[]{:S(2)}) copy-start(f32[2,1024]{0,1:T(8,128)} %copy.48) | copy-start | bytes 24580
  453.8 1.9 copy-start
  458.1 19.4 %copy-start.1 = (f32[1024,1024]{1,0:T(8,128)S(1)}, f32[1024,1024]{1,0:T(8,128)}, u32[]{:S(2)}) copy-start(f32[1024,1024]{1,0:T(8,128)} %copy-done) | copy-start | bytes 12582916 | tf_op jit(solution)/shard_map/cond
  525.0 3.9 copy-start.5
  799.8 7.3 copy-start.4
Sparse Core Ops, SparseCore 0:
  51.3 273.7 all-reduce.3
  529.1 270.7 all-reduce.5
where the time goes:
time: 833 us; the launch traced here: 823 us
  waiting for transfers between devices  497 us (60%)
  other arithmetic  121 us (15%)
  local copies, waits for them, and re-layouts  85.5 us (10%)
  matrix products  75.3 us (9%)
  blocking collectives  25.1 us (3%)
  between operations  18.5 us (2%)
    psum x1, waiting for transfers between devices, broadcast(): return lax.psum(block, axis)  271 us
    psum x1, waiting for transfers between devices, body(): packed_sum, diagonal_sum = lax.psum((packed, diagonal), 'fsdp')  226 us
    another operation x3, other arithmetic, unpack_all(): jnp.stack([first_sum, second_sum], axis=1)  32.3 us
    unnamed x1, other arithmetic  28.9 us
    psum x1, blocking collectives, body(): packed_sum, diagonal_sum = lax.psum((packed, diagonal), 'fsdp')  25.1 us
    dot_general x1, matrix products, newton_root(): square = jnp.dot(factor_one, factor_one, precision=lax.Precision.HIGHEST)  19.4 us
    dot_general x1, matrix products, newton_root(): jnp.dot(jnp.sqrt(jnp.sqrt(scaling)) * factor_one, factor_two, precision=l...  18.7 us
    psum x2, local copies, waits for them, and re-layouts, body(): packed_sum, diagonal_sum = lax.psum((packed, diagonal), 'fsdp')  18.1 us
  transfers between devices with their start and end apart: 2, of which 2 were waited for; matrix products, arithmetic and copies ran while one was open for 2% of the time, Pallas kernels for 0%

commit v1 on v0

v1 whole, which is shorter than its diff:
```python
import functools

import jax
import jax.numpy as jnp
from jax import lax
from jax.experimental import pallas as pl
from jax.experimental.pallas import tpu as pltpu
from jax.sharding import PartitionSpec as P

BLOCK = 1024
damping = 0.01
TILE = 256
STRIP = 128
STRIPS = BLOCK // STRIP
TILES = BLOCK // TILE
MESH = pl.DeviceIdType.MESH


def eye_strip(row0, rows, columns):
    row = lax.broadcasted_iota(jnp.int32, (rows, columns), 0) + row0
    column = lax.broadcasted_iota(jnp.int32, (rows, columns), 1)
    return (row == column).astype(jnp.float32)


def dot(a, b):
    return jnp.dot(a, b, preferred_element_type=jnp.float32)


def nearest_order(total):
    return [sorted(range(total), key=lambda k: (abs(k - b), k)) for b in range(total)]


def kernel(n, total, tp_total, count_ref, mine_ref, g_ref, update_ref, owned_ref, rows, gram, wide,
           low_a, low_b, low_x, roots, in_send, in_recv, up_send, down_send, mate_send, root_recv):
    me = lax.axis_index("fsdp")
    tp = lax.axis_index("tp")
    stride = n // total
    lane = lax.rem(tp, stride)
    home = me // stride
    is_home = lax.rem(me, stride) == lane

    def to(device):
        return {"fsdp": device}

    barrier = pltpu.get_barrier_semaphore()

    @pl.loop(1, n)
    def _(d):
        pl.semaphore_signal(barrier, inc=1, device_id=to(lax.rem(me + d, n)), device_id_type=MESH)

    pl.semaphore_wait(barrier, n - 1)

    def row_copy(block, source, target):
        return pltpu.make_async_remote_copy(
            src_ref=g_ref.at[block], dst_ref=rows.at[source], send_sem=in_send.at[block],
            recv_sem=in_recv.at[source], device_id=to(target), device_id_type=MESH)

    for block in range(total):
        target = stride * block + lane

        @pl.when(me != target)
        def _():
            row_copy(block, me, target).start()

    def strip_copy(k, s, target, send_sem):
        piece = roots.at[k, pl.ds(s * STRIP, STRIP), pl.ds(0, (s + 1) * STRIP)]
        return pltpu.make_async_remote_copy(
            src_ref=piece, dst_ref=piece, send_sem=send_sem, recv_sem=root_recv.at[k, s],
            device_id=to(target), device_id_type=MESH)

    def up_copy(k, s):
        return strip_copy(k, s, me + stride, up_send.at[k, s])

    def down_copy(k, s):
        return strip_copy(k, s, me - stride, down_send.at[k, s])

    def mate_copy(m, k, s):
        mate = stride * home + lax.rem(lane + 1 + m, stride)
        return strip_copy(k, s, mate, mate_send.at[m, k, s])

    def pass_on(k, s):
        for m in range(stride - 1):
            mate_copy(m, k, s).start()

        @pl.when((k <= home) & (home < total - 1))
        def _():
            up_copy(k, s).start()

        @pl.when((k >= home) & (home > 0))
        def _():
            down_copy(k, s).start()

    @pl.when(is_home)
    def _():
        def add_rows(read, first):
            @pl.loop(0, TILES)
            def _(i):
                at = pl.ds(pl.multiple_of(i * TILE, TILE), TILE)
                term = lax.dot_general(read(at), read(slice(None)), (((0,), (0,)), ((), ())),
                                       preferred_element_type=jnp.float32)
                gram[at, :] = term if first else gram[at, :] + term

        add_rows(lambda at: g_ref[home, :, at], True)

        @pl.loop(1, n)
        def _(d):
            source = lax.rem(me + d, n)
            row_copy(home, source, me).wait_recv()
            add_rows(lambda at: rows[source, :, at], False)

        inverse = 1.0 / jnp.full((1, 1), count_ref[0], jnp.float32)

        def statistic(i, squares):
            row0 = pl.multiple_of(i * TILE, TILE)
            at = pl.ds(row0, TILE)
            value = gram[at, :] * inverse + damping * eye_strip(row0, TILE, BLOCK)
            gram[at, :] = value
            return squares + jnp.sum(value * value, axis=0, keepdims=True)

        squares = lax.fori_loop(0, TILES, statistic, jnp.zeros((1, BLOCK), jnp.float32))
        scaling = 2.5 / jnp.sqrt(jnp.sum(squares, axis=1, keepdims=True))
        quarter = jnp.sqrt(jnp.sqrt(scaling))

        @pl.loop(0, TILES)
        def _(i):
            at = pl.ds(pl.multiple_of(i * TILE, TILE), TILE)
            scaled = gram[at, :] * scaling
            gram[at, :] = scaled
            low_a[at, :] = scaled.astype(jnp.bfloat16)

        @pl.loop(0, TILES)
        def _(i):
            at = pl.ds(pl.multiple_of(i * TILE, TILE), TILE)
            second = dot(low_a[at, :], low_a[...])
            scaled = gram[at, :]
            low_b[at, :] = (second * 0.0625 - 0.625 * scaled).astype(jnp.bfloat16)
            value = 1.25 * scaled - 0.25 * second
            wide[at, :] = value
            low_x[at, :] = value.astype(jnp.bfloat16)

        @pl.loop(0, TILES)
        def _(i):
            at = pl.ds(pl.multiple_of(i * TILE, TILE), TILE)
            value = 1.5625 * wide[at, :] + dot(low_b[at, :], low_x[...])
            wide[at, :] = value
            low_a[at, :] = value.astype(jnp.bfloat16)

        for i in range(TILES):
            at = pl.ds(i * TILE, TILE)
            width = (i + 1) * TILE
            value = 1.5625 * wide[at, :width] + dot(low_b[at, :], low_a[:, :width])
            value = 1.5625 * eye_strip(i * TILE, TILE, width) - 0.3125 * gram[at, :width] - 0.25 * value
            roots[home, at, pl.ds(0, width)] = (quarter * value).astype(jnp.bfloat16)
            for s in range(i * TILE // STRIP, (i + 1) * TILE // STRIP):
                pass_on(home, s)

    owned_ref[...] = jnp.zeros_like(owned_ref)
    order = nearest_order(total)

    @pl.loop(0, total)
    def _(step):
        k = jnp.int32(0)
        for b in range(total):
            for i in range(total):
                k = jnp.where((home == b) & (step == i), order[b][i], k)

        @pl.when(jnp.logical_not(is_home & (step == 0)))
        def _():
            for s in range(STRIPS):
                strip_copy(k, s, me, up_send.at[k, s]).wait_recv()

                @pl.when(is_home)
                def _():
                    pass_on(k, s)

        def mirror(row0, column0, size):
            piece = roots[k, pl.ds(row0, size), pl.ds(column0, size)]
            turned = piece.astype(jnp.float32).T.astype(jnp.bfloat16)
            roots[k, pl.ds(column0, size), pl.ds(row0, size)] = turned

        for i in range(TILES):
            mirror(i * TILE + STRIP, i * TILE, STRIP)
            for j in range(i):
                mirror(i * TILE, j * TILE, TILE)
        mine = mine_ref[k]

        @pl.loop(0, TILES)
        def _(i):
            at = pl.ds(pl.multiple_of(i * TILE, TILE), TILE)
            update_ref[k, :, at] = dot(g_ref[k], roots[k, :, at]).astype(jnp.bfloat16)
            held = owned_ref[at, :].astype(jnp.float32) + roots[k, at, :].astype(jnp.float32) * mine
            owned_ref[at, :] = held.astype(jnp.bfloat16)

    for block in range(total):
        target = stride * block + lane

        @pl.when(me != target)
        def _():
            row_copy(block, me, target).wait_send()

    @pl.when(is_home)
    def _():
        @pl.loop(0, total)
        def _(k):
            for s in range(STRIPS):
                for m in range(stride - 1):
                    mate_copy(m, k, s).wait_send()

                @pl.when((k <= home) & (home < total - 1))
                def _():
                    up_copy(k, s).wait_send()

                @pl.when((k >= home) & (home > 0))
                def _():
                    down_copy(k, s).wait_send()


def body(n, tp_total, gradients, row_counts, block_owner):
    fsdp_index = lax.axis_index("fsdp")
    tp_index = lax.axis_index("tp")
    layers, row_slots, columns = gradients.shape
    per_device = columns // BLOCK
    total = layers * per_device
    stride = n // total
    limit = row_counts[fsdp_index]
    valid_rows = (jnp.arange(row_slots, dtype=jnp.int32) < limit).astype(jnp.bfloat16)
    masked = gradients * valid_rows[None, :, None]
    blocked = masked.reshape(layers, row_slots, per_device, BLOCK).transpose(0, 2, 1, 3)
    blocked = blocked.reshape(total, row_slots, BLOCK)
    total_rows = jnp.sum(row_counts).astype(jnp.float32).reshape(1)
    local_owner = lax.dynamic_slice(
        block_owner, (jnp.int32(0), tp_index * per_device), (layers, per_device)
    ).reshape(total)
    mine = (local_owner == fsdp_index).astype(jnp.float32)
    vmem = pl.BlockSpec(memory_space=pltpu.VMEM)
    smem = pl.BlockSpec(memory_space=pltpu.SMEM)
    square = (BLOCK, BLOCK)
    dma = pltpu.SemaphoreType.DMA
    update, owned = pl.pallas_call(
        functools.partial(kernel, n, total, tp_total),
        out_shape=(
            jax.ShapeDtypeStruct((total, row_slots, BLOCK), jnp.bfloat16),
            jax.ShapeDtypeStruct(square, jnp.bfloat16),
        ),
        in_specs=[smem, smem, vmem],
        out_specs=(vmem, vmem),
        scratch_shapes=[
            pltpu.VMEM((n, row_slots, BLOCK), jnp.bfloat16),
            pltpu.VMEM(square, jnp.float32),
            pltpu.VMEM(square, jnp.float32),
            pltpu.VMEM(square, jnp.bfloat16),
            pltpu.VMEM(square, jnp.bfloat16),
            pltpu.VMEM(square, jnp.bfloat16),
            pltpu.VMEM((total,) + square, jnp.bfloat16),
            dma((total,)),
            dma((n,)),
            dma((total, STRIPS)),
            dma((total, STRIPS)),
            dma((max(stride - 1, 1), total, STRIPS)),
            dma((total, STRIPS)),
        ],
        compiler_params=pltpu.CompilerParams(
            collective_id=0, has_side_effects=True, vmem_limit_bytes=56 * 2**20
        ),
    )(total_rows, mine, blocked)
    update = update.reshape(layers, per_device, row_slots, BLOCK).transpose(0, 2, 1, 3)
    return update.reshape(layers, row_slots, columns), owned


def solution(mesh):
    placed = (P(None, "fsdp", "tp"), P(), P())
    return jax.shard_map(
        functools.partial(body, mesh.shape["fsdp"], mesh.shape["tp"]),
        mesh=mesh,
        in_specs=placed,
        out_specs=(P(None, "fsdp", "tp"), P("fsdp", "tp")),
        check_vma=False,
    )
```

time: 833 us -> 141 us (0.17)
  the two profiles are of different devices: /device:TPU:0 before, /device:TPU:9 now
where the time goes in v1:
time: 141 us
  Pallas kernels  127 us (90%)
  local copies, waits for them, and re-layouts  6.71 us (5%)
  other arithmetic  5.9 us (4%)
    pallas_call x1, Pallas kernels, body(): pl.pallas_call(functools.partial(kernel, n, total, tp_total), out_shape=(...  127 us
    reshape x1, local copies, waits for them, and re-layouts, body(): return (update.reshape(layers, row_slots, columns), owned)  3.3 us

profile of v1, /device:TPU:9, one launch (start us, length us, event | category | flops | bytes accessed | tf_op | source)
XLA Modules:
  0.0 141.2 jit_solution(12060269052710658134)
XLA Ops:
  0.6 1.2 dynamic_slice.7
  1.9 1.3 reduce_sum.9
  3.8 0.6 compare_convert_fusion
  4.4 0.8 compare_convert_fusion.1
  5.1 0.6 reshape.31.mine_ref
  5.8 1.8 %broadcast_multiply_fusion = bf16[2,256,2048]{2,1,0:T(8,128)(2,1)S(1)} fusion(bf16[2,256,2048]{2,1,0:T(8,128)(2,1)} %param.3, bf16[256]{0:T(256)(128)(2,1)S(1)} %compare_convert_fusion), kind=kLoop, calls=%fused_computation.1 | loop fusion | flops 1048576 | bytes 4194816 | tf_op jit(solution)/shard_map/mul | solution.py:227
  7.6 0.2 fusion
  7.8 1.5 %pad_maximum_fusion = bf16[2,512,1024]{2,1,0:T(8,128)(2,1)} fusion(bf16[2,256,1024]{2,1,0:T(8,128)(2,1)S(1)} %get-tuple-element.7, bf16[2,256,1024]{2,1,0:T(8,128)(2,1)S(1)} %get-tuple-element.6), kind=kLoop, calls=%fused_computation | loop fusion | flops 4194304 | bytes 4194304 | tf_op jit(solution)/shard_map/concatenate
  9.3 127.3 %shard_map.50 = (bf16[4,256,1024]{2,1,0:T(8,128)(2,1)}, bf16[1024,1024]{1,0:T(8,128)(2,1)}) custom-call(f32[1]{0:T(128)} %bitcast.count_ref, f32[4]{0:T(128)} %reshape.31.mine_ref, bf16[4,256,1024]{2,1,0:T(8,128)(2,1)} %bitcast.8), custom_call_target="tpu_custom_call" | custom-call | tf_op jit(solution)/shard_map/pallas_call | solution.py:239
  136.6 0.0 copy-start
  136.6 3.3 %copy.6 = bf16[2,2,32,8,1024]{4,3,1,2,0:T(8,128)(2,1)} copy(bf16[2,2,32,8,1024]{4,3,2,1,0:T(8,128)(2,1)} %bitcast.10) | data formatting | bytes 4194304 | tf_op jit(solution)/shard_map/reshape | solution.py:267
  139.9 0.0 copy-done
  139.9 1.3 copy.8
Async XLA Ops:
  136.6 3.3 %copy-start = (bf16[1024,1024]{1,0:T(8,128)(2,1)S(1)}, bf16[1024,1024]{1,0:T(8,128)(2,1)}, u32[]{:S(2)}) copy-start(bf16[1024,1024]{1,0:T(8,128)(2,1)} %get-tuple-element.11) | copy-start | bytes 6291460

commit v2 on v1

v2 whole, which is shorter than its diff:
```python
import functools

import jax
import jax.numpy as jnp
from jax import lax
from jax.experimental import pallas as pl
from jax.experimental.pallas import tpu as pltpu
from jax.sharding import PartitionSpec as P

BLOCK = 1024
damping = 0.01
TILE = 256
STRIP = 128
STRIPS = BLOCK // STRIP
TILES = BLOCK // TILE
MESH = pl.DeviceIdType.MESH


def eye_strip(row0, rows, columns):
    row = lax.broadcasted_iota(jnp.int32, (rows, columns), 0) + row0
    column = lax.broadcasted_iota(jnp.int32, (rows, columns), 1)
    return (row == column).astype(jnp.float32)


def dot(a, b):
    return jnp.dot(a, b, preferred_element_type=jnp.float32)


def arrange(total):
    place = sorted(range(total), key=lambda p: (abs(2 * p - total + 1), p))
    early = place[: total // 2]
    order = [sorted(range(total), key=lambda p: (p not in early, abs(p - h), p)) for h in range(total)]
    return place, order


def pick(index, table):
    value = jnp.int32(table[0])
    for i, entry in enumerate(table[1:], 1):
        value = jnp.where(index == i, entry, value)
    return value


def kernel(n, total, count_ref, owner_ref, g_ref, update_ref, owned_ref, masked, rows, gram, wide,
           low_a, low_b, low_x, roots, in_send, in_recv, home_send, up_send, down_send, mate_send, root_recv):
    me = lax.axis_index("fsdp")
    tp = lax.axis_index("tp")
    layers, row_slots, columns = g_ref.shape
    per_device = columns // BLOCK
    half = row_slots // 2
    stride = n // total
    lane = lax.rem(tp, stride)
    relay = lax.rem(lane + 1, stride)
    home = me // stride
    is_home = lax.rem(me, stride) == lane
    is_relay = lax.rem(me, stride) == relay
    place, order = arrange(total)
    early = total // 2
    block_at = [place.index(p) for p in range(total)]
    home_block = pick(home, block_at)
    is_early = is_home & (home_block < early)

    def to(device):
        return {"fsdp": device}

    barrier = pltpu.get_barrier_semaphore()

    @pl.loop(1, n)
    def _(d):
        pl.semaphore_signal(barrier, inc=1, device_id=to(lax.rem(me + d, n)), device_id_type=MESH)

    limit = count_ref[me]
    valid = lax.broadcasted_iota(jnp.int32, (row_slots, BLOCK), 0) < limit
    valid = jnp.where(valid, 1.0, 0.0).astype(jnp.bfloat16)
    for block in range(total):
        column0 = block % per_device * BLOCK
        masked[block] = g_ref[block // per_device, :, column0:column0 + BLOCK] * valid

    pl.semaphore_wait(barrier, n - 1)

    def row_copy(block, part, source, target):
        return pltpu.make_async_remote_copy(
            src_ref=masked.at[block, pl.ds(part * half, half)],
            dst_ref=rows.at[part, pl.ds(pl.multiple_of(source * half, half), half)],
            send_sem=in_send.at[block, part],
            recv_sem=in_recv.at[part, source], device_id=to(target), device_id_type=MESH)

    def each_send(blocks, act):
        for part in range(2):
            for block in blocks:
                target = stride * place[block] + lane

                @pl.when(me != target)
                def _():
                    act(row_copy(block, part, me, target))

    def second_sends():
        each_send(range(early), lambda copy: copy.wait_send())
        each_send(range(early, total), lambda copy: copy.start())

    each_send(range(early), lambda copy: copy.start())

    @pl.when(jnp.logical_not(is_early))
    def _():
        second_sends()

    def strip_copy(k, s, target, send_sem):
        piece = roots.at[k, pl.ds(s * STRIP, STRIP), pl.ds(0, (s + 1) * STRIP)]
        return pltpu.make_async_remote_copy(
            src_ref=piece, dst_ref=piece, send_sem=send_sem, recv_sem=root_recv.at[k, s],
            device_id=to(target), device_id_type=MESH)

    def home_copy(s):
        return strip_copy(home, s, stride * home + relay, home_send.at[s])

    def each_pass(k, s, act):
        for m in range(stride - 1):
            mate = stride * home + lax.rem(relay + 1 + m, stride)
            copy = strip_copy(k, s, mate, mate_send.at[m, k, s])
            if m < stride - 2:
                act(copy)
            else:
                @pl.when(k != home)
                def _():
                    act(copy)

        @pl.when((k <= home) & (home < total - 1))
        def _():
            act(strip_copy(k, s, me + stride, up_send.at[k, s]))

        @pl.when((k >= home) & (home > 0))
        def _():
            act(strip_copy(k, s, me - stride, down_send.at[k, s]))

    @pl.when(is_home)
    def _():
        def add_rows(part):
            mine_at = pl.ds(pl.multiple_of(me * half, half), half)
            rows[part, mine_at, :] = masked[home_block, part * half:(part + 1) * half, :]

            @pl.loop(1, n)
            def _(d):
                source = lax.rem(me + d, n)
                row_copy(home_block, part, source, me).wait_recv()

            @pl.loop(0, TILES)
            def _(i):
                at = pl.ds(pl.multiple_of(i * TILE, TILE), TILE)
                term = lax.dot_general(rows[part, :, at], rows[part], (((0,), (0,)), ((), ())),
                                       preferred_element_type=jnp.float32)
                gram[at, :] = term if part == 0 else gram[at, :] + term

        add_rows(0)

        @pl.when(is_early)
        def _():
            second_sends()

        add_rows(1)
        count = count_ref[0]
        for i in range(1, n):
            count = count + count_ref[i]
        total_rows = jnp.full((1, 1), count, jnp.int32).astype(jnp.float32)
        inverse = 1.0 / total_rows

        def statistic(i, squares):
            row0 = pl.multiple_of(i * TILE, TILE)
            at = pl.ds(row0, TILE)
            value = gram[at, :] * inverse + damping * eye_strip(row0, TILE, BLOCK)
            gram[at, :] = value
            return squares + jnp.sum(value * value, axis=0, keepdims=True)

        squares = lax.fori_loop(0, TILES, statistic, jnp.zeros((1, BLOCK), jnp.float32))
        scaling = 2.5 / jnp.sqrt(jnp.sum(squares, axis=1, keepdims=True))
        quarter = jnp.sqrt(jnp.sqrt(scaling))

        @pl.loop(0, TILES)
        def _(i):
            at = pl.ds(pl.multiple_of(i * TILE, TILE), TILE)
            scaled = gram[at, :] * scaling
            gram[at, :] = scaled
            low_a[at, :] = scaled.astype(jnp.bfloat16)

        @pl.loop(0, TILES)
        def _(i):
            at = pl.ds(pl.multiple_of(i * TILE, TILE), TILE)
            second = dot(low_a[at, :], low_a[...])
            scaled = gram[at, :]
            low_b[at, :] = (second * 0.0625 - 0.625 * scaled).astype(jnp.bfloat16)
            value = 1.25 * scaled - 0.25 * second
            wide[at, :] = value
            low_x[at, :] = value.astype(jnp.bfloat16)

        @pl.loop(0, TILES)
        def _(i):
            at = pl.ds(pl.multiple_of(i * TILE, TILE), TILE)
            value = 1.5625 * wide[at, :] + dot(low_b[at, :], low_x[...])
            wide[at, :] = value
            low_a[at, :] = value.astype(jnp.bfloat16)

        for i in range(TILES):
            at = pl.ds(i * TILE, TILE)
            width = (i + 1) * TILE
            value = 1.5625 * wide[at, :width] + dot(low_b[at, :], low_a[:, :width])
            value = 1.5625 * eye_strip(i * TILE, TILE, width) - 0.3125 * gram[at, :width] - 0.25 * value
            roots[home, at, pl.ds(0, width)] = (quarter * value).astype(jnp.bfloat16)
            for s in range(i * TILE // STRIP, (i + 1) * TILE // STRIP):
                home_copy(s).start()

    owned_ref[...] = jnp.zeros_like(owned_ref)

    @pl.loop(0, total)
    def _(step):
        k = pick(home * total + step, [p for line in order for p in line])

        @pl.when(jnp.logical_not(is_home & (k == home)))
        def _():
            for s in range(STRIPS):
                strip_copy(k, s, me, home_send.at[s]).wait_recv()

                @pl.when(is_relay)
                def _():
                    each_pass(k, s, lambda copy: copy.start())

        def mirror(row0, column0, size):
            piece = roots[k, pl.ds(row0, size), pl.ds(column0, size)]
            turned = piece.astype(jnp.float32).T.astype(jnp.bfloat16)
            roots[k, pl.ds(column0, size), pl.ds(row0, size)] = turned

        for i in range(TILES):
            mirror(i * TILE + STRIP, i * TILE, STRIP)
            for j in range(i):
                mirror(i * TILE, j * TILE, TILE)
        block = pick(k, block_at)
        layer = block // per_device
        column = lax.rem(block, per_device)
        owner = owner_ref[layer, tp * per_device + column]
        mine = jnp.where(owner == me, 1.0, 0.0)

        @pl.loop(0, TILES)
        def _(i):
            at = pl.ds(pl.multiple_of(i * TILE, TILE), TILE)
            out_at = pl.ds(pl.multiple_of(column * BLOCK + i * TILE, TILE), TILE)
            update_ref[layer, :, out_at] = dot(masked[block], roots[k, :, at]).astype(jnp.bfloat16)
            held = owned_ref[at, :].astype(jnp.float32) + roots[k, at, :].astype(jnp.float32) * mine
            owned_ref[at, :] = held.astype(jnp.bfloat16)

    each_send(range(early, total), lambda copy: copy.wait_send())

    @pl.when(is_home)
    def _():
        for s in range(STRIPS):
            home_copy(s).wait_send()

    @pl.when(is_relay)
    def _():
        @pl.loop(0, total)
        def _(k):
            for s in range(STRIPS):
                each_pass(k, s, lambda copy: copy.wait_send())


def body(n, gradients, row_counts, block_owner):
    layers, row_slots, columns = gradients.shape
    total = layers * (columns // BLOCK)
    stride = n // total
    vmem = pl.BlockSpec(memory_space=pltpu.VMEM)
    smem = pl.BlockSpec(memory_space=pltpu.SMEM)
    square = (BLOCK, BLOCK)
    dma = pltpu.SemaphoreType.DMA
    return pl.pallas_call(
        functools.partial(kernel, n, total),
        out_shape=(
            jax.ShapeDtypeStruct(gradients.shape, jnp.bfloat16),
            jax.ShapeDtypeStruct(square, jnp.bfloat16),
        ),
        in_specs=[smem, smem, vmem],
        out_specs=(vmem, vmem),
        scratch_shapes=[
            pltpu.VMEM((total, row_slots, BLOCK), jnp.bfloat16),
            pltpu.VMEM((2, n * row_slots // 2, BLOCK), jnp.bfloat16),
            pltpu.VMEM(square, jnp.float32),
            pltpu.VMEM(square, jnp.float32),
            pltpu.VMEM(square, jnp.bfloat16),
            pltpu.VMEM(square, jnp.bfloat16),
            pltpu.VMEM(square, jnp.bfloat16),
            pltpu.VMEM((total,) + square, jnp.bfloat16),
            dma((total, 2)),
            dma((2, n)),
            dma((STRIPS,)),
            dma((total, STRIPS)),
            dma((total, STRIPS)),
            dma((stride - 1, total, STRIPS)),
            dma((total, STRIPS)),
        ],
        compiler_params=pltpu.CompilerParams(
            collective_id=0, has_side_effects=True, vmem_limit_bytes=56 * 2**20
        ),
    )(row_counts, block_owner, gradients)


def solution(mesh):
    placed = (P(None, "fsdp", "tp"), P(), P())
    return jax.shard_map(
        functools.partial(body, mesh.shape["fsdp"]),
        mesh=mesh,
        in_specs=placed,
        out_specs=(P(None, "fsdp", "tp"), P("fsdp", "tp")),
        check_vma=False,
    )
```

time: 141 us -> 143 us (1.014)
  the two profiles are of different devices: /device:TPU:9 before, /device:TPU:0 now
where the time goes in v2:
time: 143 us
  Pallas kernels  137 us (96%)
  local copies, waits for them, and re-layouts  4.63 us (3%)
    pallas_call x1, Pallas kernels, body(): pl.pallas_call(functools.partial(kernel, n, total), out_shape=(jax.ShapeD...  137 us
    unnamed x4, local copies, waits for them, and re-layouts  4.63 us

profile of v2, /device:TPU:0, one launch (start us, length us, event | category | flops | bytes accessed | tf_op | source)
XLA Modules:
  0.0 142.6 jit_solution(14600824243787951361)
XLA Ops:
  0.6 137.3 %shard_map.50 = (bf16[2,256,2048]{2,1,0:T(8,128)(2,1)}, bf16[1024,1024]{1,0:T(8,128)(2,1)}) custom-call(s32[8]{0:T(128)} %count_ref.1, s32[2,8]{1,0:T(2,128)} %owner_ref.1, bf16[2,256,2048]{2,1,0:T(8,128)(2,1)} %g_ref.1), custom_call_target="tpu_custom_call" | custom-call | tf_op jit(solution)/shard_map/pallas_call | solution.py:270
  138.0 0.0 copy-start
  138.0 3.3 %copy.7 = bf16[2,256,2048]{2,1,0:T(8,128)(2,1)} copy(bf16[2,256,2048]{2,1,0:T(8,128)(2,1)} %get-tuple-element.4) | data formatting | bytes 4194304
  141.3 0.0 copy-done
  141.3 1.3 copy.8
Async XLA Ops:
  138.0 3.3 %copy-start = (bf16[1024,1024]{1,0:T(8,128)(2,1)S(1)}, bf16[1024,1024]{1,0:T(8,128)(2,1)}, u32[]{:S(2)}) copy-start(bf16[1024,1024]{1,0:T(8,128)(2,1)} %get-tuple-element.5) | copy-start | bytes 6291460

commit v3 on v2

--- a/solution.py
+++ b/solution.py
@@ -13,6 +13,7 @@
 STRIP = 128
 STRIPS = BLOCK // STRIP
 TILES = BLOCK // TILE
+CHUNK = 16
 MESH = pl.DeviceIdType.MESH
 
 
@@ -41,7 +42,7 @@
 
 
 def kernel(n, total, count_ref, owner_ref, g_ref, update_ref, owned_ref, masked, rows, gram, wide,
-           low_a, low_b, low_x, roots, in_send, in_recv, home_send, up_send, down_send, mate_send, root_recv):
+           product, low_a, low_b, low_x, roots, in_send, in_recv, home_send, up_send, down_send, mate_send, root_recv):
     me = lax.axis_index("fsdp")
     tp = lax.axis_index("tp")
     layers, row_slots, columns = g_ref.shape
@@ -69,11 +70,16 @@
         pl.semaphore_signal(barrier, inc=1, device_id=to(lax.rem(me + d, n)), device_id_type=MESH)
 
     limit = count_ref[me]
-    valid = lax.broadcasted_iota(jnp.int32, (row_slots, BLOCK), 0) < limit
-    valid = jnp.where(valid, 1.0, 0.0).astype(jnp.bfloat16)
-    for block in range(total):
-        column0 = block % per_device * BLOCK
-        masked[block] = g_ref[block // per_device, :, column0:column0 + BLOCK] * valid
+
+    @pl.loop(0, row_slots // CHUNK)
+    def _(c):
+        row0 = pl.multiple_of(c * CHUNK, CHUNK)
+        at = pl.ds(row0, CHUNK)
+        valid = lax.broadcasted_iota(jnp.int32, (CHUNK, BLOCK), 0) + row0 < limit
+        valid = jnp.where(valid, 1.0, 0.0).astype(jnp.bfloat16)
+        for block in range(total):
+            column0 = block % per_device * BLOCK
+            masked[block, at, :] = g_ref[block // per_device, at, column0:column0 + BLOCK] * valid
 
     pl.semaphore_wait(barrier, n - 1)
 
@@ -133,7 +139,7 @@
 
     @pl.when(is_home)
     def _():
-        def add_rows(part):
+        def take_rows(part):
             mine_at = pl.ds(pl.multiple_of(me * half, half), half)
             rows[part, mine_at, :] = masked[home_block, part * half:(part + 1) * half, :]
 
@@ -142,67 +148,110 @@
                 source = lax.rem(me + d, n)
                 row_copy(home_block, part, source, me).wait_recv()
 
-            @pl.loop(0, TILES)
-            def _(i):
-                at = pl.ds(pl.multiple_of(i * TILE, TILE), TILE)
-                term = lax.dot_general(rows[part, :, at], rows[part], (((0,), (0,)), ((), ())),
-                                       preferred_element_type=jnp.float32)
-                gram[at, :] = term if part == 0 else gram[at, :] + term
-
-        add_rows(0)
+        def gram_strip(part, at):
+            return lax.dot_general(rows[part, :, at], rows[part], (((0,), (0,)), ((), ())),
+                                   preferred_element_type=jnp.float32)
+
+        def strips(act, start=0):
+            return lax.fori_loop(0, TILES, lambda i, x: act(pl.multiple_of(i * TILE, TILE), x), start)
+
+        def chunks(row0, act, start=0):
+            def step(c, x):
+                first = pl.multiple_of(c * CHUNK, CHUNK)
+                return act(pl.ds(first, CHUNK), pl.ds(pl.multiple_of(row0 + first, CHUNK), CHUNK), x)
+
+            return lax.fori_loop(0, TILE // CHUNK, step, start)
+
+        take_rows(0)
+
+        def first_half(row0, x):
+            at = pl.ds(row0, TILE)
+            gram[at, :] = gram_strip(0, at)
+            return x
+
+        strips(first_half)
 
         @pl.when(is_early)
         def _():
             second_sends()
 
-        add_rows(1)
+        take_rows(1)
         count = count_ref[0]
         for i in range(1, n):
             count = count + count_ref[i]
-        total_rows = jnp.full((1, 1), count, jnp.int32).astype(jnp.float32)
-        inverse = 1.0 / total_rows
-
-        def statistic(i, squares):
-            row0 = pl.multiple_of(i * TILE, TILE)
+        inverse = 1.0 / jnp.full((1, 1), count, jnp.int32).astype(jnp.float32)
+
+        def statistic(row0, squares):
             at = pl.ds(row0, TILE)
-            value = gram[at, :] * inverse + damping * eye_strip(row0, TILE, BLOCK)
-            gram[at, :] = value
-            return squares + jnp.sum(value * value, axis=0, keepdims=True)
-
-        squares = lax.fori_loop(0, TILES, statistic, jnp.zeros((1, BLOCK), jnp.float32))
+            product[...] = gram_strip(1, at)
+
+            def step(near, far, squares):
+                value = (gram[far, :] + product[near, :]) * inverse
+                gram[far, :] = value
+                low_a[far, :] = value.astype(jnp.bfloat16)
+                value = value * value
+                return squares + value[:8] + value[8:]
+
+            squares = chunks(row0, step, squares)
+            eye = eye_strip(0, TILE, TILE)
+            value = gram[at, at]
+            extra = eye * (2.0 * damping * value + damping * damping)
+            value = value + damping * eye
+            gram[at, at] = value
+            low_a[at, at] = value.astype(jnp.bfloat16)
+            extra = jnp.sum(extra.reshape(TILE // 8, 8, TILE), axis=0)
+            return squares + jnp.concatenate([extra] + [jnp.zeros_like(extra)] * (TILES - 1), axis=1)
+
+        squares = strips(statistic, jnp.zeros((8, BLOCK), jnp.float32))
+        squares = jnp.sum(squares, axis=0, keepdims=True)
         scaling = 2.5 / jnp.sqrt(jnp.sum(squares, axis=1, keepdims=True))
         quarter = jnp.sqrt(jnp.sqrt(scaling))
 
-        @pl.loop(0, TILES)
-        def _(i):
-            at = pl.ds(pl.multiple_of(i * TILE, TILE), TILE)
-            scaled = gram[at, :] * scaling
-            gram[at, :] = scaled
-            low_a[at, :] = scaled.astype(jnp.bfloat16)
-
-        @pl.loop(0, TILES)
-        def _(i):
-            at = pl.ds(pl.multiple_of(i * TILE, TILE), TILE)
-            second = dot(low_a[at, :], low_a[...])
-            scaled = gram[at, :]
-            low_b[at, :] = (second * 0.0625 - 0.625 * scaled).astype(jnp.bfloat16)
-            value = 1.25 * scaled - 0.25 * second
-            wide[at, :] = value
-            low_x[at, :] = value.astype(jnp.bfloat16)
-
-        @pl.loop(0, TILES)
-        def _(i):
-            at = pl.ds(pl.multiple_of(i * TILE, TILE), TILE)
-            value = 1.5625 * wide[at, :] + dot(low_b[at, :], low_x[...])
-            wide[at, :] = value
-            low_a[at, :] = value.astype(jnp.bfloat16)
+        def second_power(row0, x):
+            product[...] = dot(low_a[pl.ds(row0, TILE), :], low_a[...])
+
+            def step(near, far, x):
+                second = product[near, :] * (scaling * scaling)
+                scaled = gram[far, :] * scaling
+                gram[far, :] = scaled
+                low_b[far, :] = (0.0625 * second - 0.625 * scaled).astype(jnp.bfloat16)
+                value = 1.25 * scaled - 0.25 * second
+                wide[far, :] = value
+                low_x[far, :] = value.astype(jnp.bfloat16)
+                return x
+
+            return chunks(row0, step, x)
+
+        strips(second_power)
+
+        def third_power(row0, x):
+            product[...] = dot(low_b[pl.ds(row0, TILE), :], low_x[...])
+
+            def step(near, far, x):
+                value = 1.5625 * wide[far, :] + product[near, :]
+                wide[far, :] = value
+                low_a[far, :] = value.astype(jnp.bfloat16)
+                return x
+
+            return chunks(row0, step, x)
+
+        strips(third_power)
 
         for i in range(TILES):
             at = pl.ds(i * TILE, TILE)
             width = (i + 1) * TILE
-            value = 1.5625 * wide[at, :width] + dot(low_b[at, :], low_a[:, :width])
-            value = 1.5625 * eye_strip(i * TILE, TILE, width) - 0.3125 * gram[at, :width] - 0.25 * value
-            roots[home, at, pl.ds(0, width)] = (quarter * value).astype(jnp.bfloat16)
+            product[:, :width] = dot(low_b[at, :], low_a[:, :width])
+
+            def step(near, far, x, width=width):
+                value = 1.5625 * wide[far, :width] + product[near, :width]
+                value = quarter * (-0.3125 * gram[far, :width] - 0.25 * value)
+                wide[far, :width] = value
+                roots[home, far, :width] = value.astype(jnp.bfloat16)
+                return x
+
+            chunks(i * TILE, step, 0)
+            value = wide[at, at] + quarter * (1.5625 * eye_strip(0, TILE, TILE))
+            roots[home, at, at] = value.astype(jnp.bfloat16)
             for s in range(i * TILE // STRIP, (i + 1) * TILE // STRIP):
                 home_copy(s).start()
 
@@ -223,8 +272,7 @@
 
         def mirror(row0, column0, size):
             piece = roots[k, pl.ds(row0, size), pl.ds(column0, size)]
-            turned = piece.astype(jnp.float32).T.astype(jnp.bfloat16)
-            roots[k, pl.ds(column0, size), pl.ds(row0, size)] = turned
+            roots[k, pl.ds(column0, size), pl.ds(row0, size)] = piece.T
 
         for i in range(TILES):
             mirror(i * TILE + STRIP, i * TILE, STRIP)
@@ -234,15 +282,13 @@
         layer = block // per_device
         column = lax.rem(block, per_device)
         owner = owner_ref[layer, tp * per_device + column]
-        mine = jnp.where(owner == me, 1.0, 0.0)
 
         @pl.loop(0, TILES)
         def _(i):
             at = pl.ds(pl.multiple_of(i * TILE, TILE), TILE)
             out_at = pl.ds(pl.multiple_of(column * BLOCK + i * TILE, TILE), TILE)
             update_ref[layer, :, out_at] = dot(masked[block], roots[k, :, at]).astype(jnp.bfloat16)
-            held = owned_ref[at, :].astype(jnp.float32) + roots[k, at, :].astype(jnp.float32) * mine
-            owned_ref[at, :] = held.astype(jnp.bfloat16)
+            owned_ref[at, :] = jnp.where(owner == me, roots[k, at, :], owned_ref[at, :])
 
     each_send(range(early, total), lambda copy: copy.wait_send())
 
@@ -280,6 +326,7 @@
             pltpu.VMEM((2, n * row_slots // 2, BLOCK), jnp.bfloat16),
             pltpu.VMEM(square, jnp.float32),
             pltpu.VMEM(square, jnp.float32),
+            pltpu.VMEM((TILE, BLOCK), jnp.float32),
             pltpu.VMEM(square, jnp.bfloat16),
             pltpu.VMEM(square, jnp.bfloat16),
             pltpu.VMEM(square, jnp.bfloat16),

time: 143 us -> 141 us (0.986)
    pallas_call x1, Pallas kernels: 137 us -> 136 us  [body(): pl.pallas_call(functools.partial(kernel, n, total), out_shape=(jax.ShapeD...]
where the time goes in v3:
time: 141 us
  Pallas kernels  136 us (96%)
  local copies, waits for them, and re-layouts  4.63 us (3%)
    pallas_call x1, Pallas kernels, body(): pl.pallas_call(functools.partial(kernel, n, total), out_shape=(jax.ShapeD...  136 us
    unnamed x4, local copies, waits for them, and re-layouts  4.63 us

profile of v3, /device:TPU:0, one launch (start us, length us, event | category | flops | bytes accessed | tf_op | source)
XLA Modules:
  0.0 140.9 jit_solution(524691609701478146)
XLA Ops:
  0.6 135.6 %shard_map.50 = (bf16[2,256,2048]{2,1,0:T(8,128)(2,1)}, bf16[1024,1024]{1,0:T(8,128)(2,1)}) custom-call(s32[8]{0:T(128)} %count_ref.1, s32[2,8]{1,0:T(2,128)} %owner_ref.1, bf16[2,256,2048]{2,1,0:T(8,128)(2,1)} %g_ref.1), custom_call_target="tpu_custom_call" | custom-call | tf_op jit(solution)/shard_map/pallas_call | solution.py:316
  136.2 0.0 copy-start
  136.2 3.3 %copy.7 = bf16[2,256,2048]{2,1,0:T(8,128)(2,1)} copy(bf16[2,256,2048]{2,1,0:T(8,128)(2,1)} %get-tuple-element.4) | data formatting | bytes 4194304
  139.5 0.0 copy-done
  139.5 1.3 copy.8
Async XLA Ops:
  136.2 3.3 %copy-start = (bf16[1024,1024]{1,0:T(8,128)(2,1)S(1)}, bf16[1024,1024]{1,0:T(8,128)(2,1)}, u32[]{:S(2)}) copy-start(bf16[1024,1024]{1,0:T(8,128)(2,1)} %get-tuple-element.5) | copy-start | bytes 6291460

commit v4 on v3

--- a/solution.py
+++ b/solution.py
@@ -14,6 +14,7 @@
 STRIPS = BLOCK // STRIP
 TILES = BLOCK // TILE
 CHUNK = 16
+DETOUR = (2, 6, 7)
 MESH = pl.DeviceIdType.MESH
 
 
@@ -25,13 +26,6 @@
 
 def dot(a, b):
     return jnp.dot(a, b, preferred_element_type=jnp.float32)
-
-
-def arrange(total):
-    place = sorted(range(total), key=lambda p: (abs(2 * p - total + 1), p))
-    early = place[: total // 2]
-    order = [sorted(range(total), key=lambda p: (p not in early, abs(p - h), p)) for h in range(total)]
-    return place, order
 
 
 def pick(index, table):
@@ -42,7 +36,7 @@
 
 
 def kernel(n, total, count_ref, owner_ref, g_ref, update_ref, owned_ref, masked, rows, gram, wide,
-           product, low_a, low_b, low_x, roots, in_send, in_recv, home_send, up_send, down_send, mate_send, root_recv):
+           product, low_a, low_b, low_x, roots, in_send, in_recv, up_send, down_send, mate_send, root_recv):
     me = lax.axis_index("fsdp")
     tp = lax.axis_index("tp")
     layers, row_slots, columns = g_ref.shape
@@ -50,15 +44,12 @@
     half = row_slots // 2
     stride = n // total
     lane = lax.rem(tp, stride)
-    relay = lax.rem(lane + 1, stride)
+    beside = lax.rem(lane + 1, stride)
     home = me // stride
     is_home = lax.rem(me, stride) == lane
-    is_relay = lax.rem(me, stride) == relay
-    place, order = arrange(total)
-    early = total // 2
-    block_at = [place.index(p) for p in range(total)]
-    home_block = pick(home, block_at)
-    is_early = is_home & (home_block < early)
+    is_beside = lax.rem(me, stride) == beside
+    upper = home >= total // 2
+    order = [sorted(range(total), key=lambda k: (abs(k - h), k)) for h in range(total)]
 
     def to(device):
         return {"fsdp": device}
@@ -90,24 +81,16 @@
             send_sem=in_send.at[block, part],
             recv_sem=in_recv.at[part, source], device_id=to(target), device_id_type=MESH)
 
-    def each_send(blocks, act):
+    def each_send(act):
         for part in range(2):
-            for block in blocks:
-                target = stride * place[block] + lane
+            for block in range(total):
+                target = stride * block + lane
 
                 @pl.when(me != target)
                 def _():
                     act(row_copy(block, part, me, target))
 
-    def second_sends():
-        each_send(range(early), lambda copy: copy.wait_send())
-        each_send(range(early, total), lambda copy: copy.start())
-
-    each_send(range(early), lambda copy: copy.start())
-
-    @pl.when(jnp.logical_not(is_early))
-    def _():
-        second_sends()
+    each_send(lambda copy: copy.start())
 
     def strip_copy(k, s, target, send_sem):
         piece = roots.at[k, pl.ds(s * STRIP, STRIP), pl.ds(0, (s + 1) * STRIP)]
@@ -115,38 +98,54 @@
             src_ref=piece, dst_ref=piece, send_sem=send_sem, recv_sem=root_recv.at[k, s],
             device_id=to(target), device_id_type=MESH)
 
-    def home_copy(s):
-        return strip_copy(home, s, stride * home + relay, home_send.at[s])
-
-    def each_pass(k, s, act):
+    def up_copy(k, s):
+        return strip_copy(k, s, me + stride, up_send.at[k, s])
+
+    def down_copy(k, s):
+        return strip_copy(k, s, me - stride, down_send.at[k, s])
+
+    def along_chain(k):
+        return (upper & (k == 0)) | (jnp.logical_not(upper) & (k == total - 1))
+
+    def home_pass(k, s, act):
+        @pl.when((k <= home) & (home < total - 1))
+        def _():
+            act(up_copy(k, s))
+
+        @pl.when((k >= home) & (home > 0))
+        def _():
+            act(down_copy(k, s))
+
         for m in range(stride - 1):
-            mate = stride * home + lax.rem(relay + 1 + m, stride)
+            mate = stride * home + lax.rem(lane + 1 + m, stride)
             copy = strip_copy(k, s, mate, mate_send.at[m, k, s])
-            if m < stride - 2:
-                act(copy)
-            else:
-                @pl.when(k != home)
+            if m == 0 and s in DETOUR:
+                @pl.when(jnp.logical_not(along_chain(k)))
                 def _():
                     act(copy)
-
-        @pl.when((k <= home) & (home < total - 1))
-        def _():
-            act(strip_copy(k, s, me + stride, up_send.at[k, s]))
-
-        @pl.when((k >= home) & (home > 0))
-        def _():
-            act(strip_copy(k, s, me - stride, down_send.at[k, s]))
+            else:
+                act(copy)
+
+    def beside_pass(k, s, act):
+        if s in DETOUR:
+            @pl.when((k == 0) & (home >= total // 2 - 1) & (home < total - 1))
+            def _():
+                act(up_copy(k, s))
+
+            @pl.when((k == total - 1) & (home <= total // 2) & (home > 0))
+            def _():
+                act(down_copy(k, s))
 
     @pl.when(is_home)
     def _():
         def take_rows(part):
             mine_at = pl.ds(pl.multiple_of(me * half, half), half)
-            rows[part, mine_at, :] = masked[home_block, part * half:(part + 1) * half, :]
+            rows[part, mine_at, :] = masked[home, part * half:(part + 1) * half, :]
 
             @pl.loop(1, n)
             def _(d):
                 source = lax.rem(me + d, n)
-                row_copy(home_block, part, source, me).wait_recv()
+                row_copy(home, part, source, me).wait_recv()
 
         def gram_strip(part, at):
             return lax.dot_general(rows[part, :, at], rows[part], (((0,), (0,)), ((), ())),
@@ -170,10 +169,6 @@
             return x
 
         strips(first_half)
-
-        @pl.when(is_early)
-        def _():
-            second_sends()
 
         take_rows(1)
         count = count_ref[0]
@@ -253,7 +248,7 @@
             value = wide[at, at] + quarter * (1.5625 * eye_strip(0, TILE, TILE))
             roots[home, at, at] = value.astype(jnp.bfloat16)
             for s in range(i * TILE // STRIP, (i + 1) * TILE // STRIP):
-                home_copy(s).start()
+                home_pass(home, s, lambda copy: copy.start())
 
     owned_ref[...] = jnp.zeros_like(owned_ref)
 
@@ -264,11 +259,15 @@
         @pl.when(jnp.logical_not(is_home & (k == home)))
         def _():
             for s in range(STRIPS):
-                strip_copy(k, s, me, home_send.at[s]).wait_recv()
-
-                @pl.when(is_relay)
+                strip_copy(k, s, me, up_send.at[k, s]).wait_recv()
+
+                @pl.when(is_home)
                 def _():
-                    each_pass(k, s, lambda copy: copy.start())
+                    home_pass(k, s, lambda copy: copy.start())
+
+                @pl.when(is_beside)
+                def _():
+                    beside_pass(k, s, lambda copy: copy.start())
 
         def mirror(row0, column0, size):
             piece = roots[k, pl.ds(row0, size), pl.ds(column0, size)]
@@ -278,31 +277,29 @@
             mirror(i * TILE + STRIP, i * TILE, STRIP)
             for j in range(i):
                 mirror(i * TILE, j * TILE, TILE)
-        block = pick(k, block_at)
-        layer = block // per_device
-        column = lax.rem(block, per_device)
+        layer = k // per_device
+        column = lax.rem(k, per_device)
         owner = owner_ref[layer, tp * per_device + column]
 
         @pl.loop(0, TILES)
         def _(i):
             at = pl.ds(pl.multiple_of(i * TILE, TILE), TILE)
             out_at = pl.ds(pl.multiple_of(column * BLOCK + i * TILE, TILE), TILE)
-            update_ref[layer, :, out_at] = dot(masked[block], roots[k, :, at]).astype(jnp.bfloat16)
+            update_ref[layer, :, out_at] = dot(masked[k], roots[k, :, at]).astype(jnp.bfloat16)
             owned_ref[at, :] = jnp.where(owner == me, roots[k, at, :], owned_ref[at, :])
 
-    each_send(range(early, total), lambda copy: copy.wait_send())
-
-    @pl.when(is_home)
-    def _():
+    each_send(lambda copy: copy.wait_send())
+
+    @pl.loop(0, total)
+    def _(k):
         for s in range(STRIPS):
-            home_copy(s).wait_send()
-
-    @pl.when(is_relay)
-    def _():
-        @pl.loop(0, total)
-        def _(k):
-            for s in range(STRIPS):
-                each_pass(k, s, lambda copy: copy.wait_send())
+            @pl.when(is_home)
+            def _():
+                home_pass(k, s, lambda copy: copy.wait_send())
+
+            @pl.when(is_beside)
+            def _():
+                beside_pass(k, s, lambda copy: copy.wait_send())
 
 
 def body(n, gradients, row_counts, block_owner):
@@ -333,7 +330,6 @@
             pltpu.VMEM((total,) + square, jnp.bfloat16),
             dma((total, 2)),
             dma((2, n)),
-            dma((STRIPS,)),
             dma((total, STRIPS)),
             dma((total, STRIPS)),
             dma((stride - 1, total, STRIPS)),

time: 141 us -> 130 us (0.922)
  the two profiles are of different devices: /device:TPU:0 before, /device:TPU:2 now
where the time goes in v4:
time: 130 us
  Pallas kernels  125 us (96%)
  local copies, waits for them, and re-layouts  4.63 us (4%)
    pallas_call x1, Pallas kernels, body(): pl.pallas_call(functools.partial(kernel, n, total), out_shape=(jax.ShapeD...  125 us
    unnamed x4, local copies, waits for them, and re-layouts  4.63 us

profile of v4, /device:TPU:2, one launch (start us, length us, event | category | flops | bytes accessed | tf_op | source)
XLA Modules:
  0.0 129.8 jit_solution(15947224065041398619)
XLA Ops:
  0.6 124.6 %shard_map.50 = (bf16[2,256,2048]{2,1,0:T(8,128)(2,1)}, bf16[1024,1024]{1,0:T(8,128)(2,1)}) custom-call(s32[8]{0:T(128)} %count_ref.1, s32[2,8]{1,0:T(2,128)} %owner_ref.1, bf16[2,256,2048]{2,1,0:T(8,128)(2,1)} %g_ref.1), custom_call_target="tpu_custom_call" | custom-call | tf_op jit(solution)/shard_map/pallas_call | solution.py:313
  125.2 0.0 copy-start
  125.2 3.3 %copy.7 = bf16[2,256,2048]{2,1,0:T(8,128)(2,1)} copy(bf16[2,256,2048]{2,1,0:T(8,128)(2,1)} %get-tuple-element.4) | data formatting | bytes 4194304
  128.5 0.0 copy-done
  128.5 1.3 %copy.8 = bf16[1024,1024]{1,0:T(8,128)(2,1)} copy(bf16[1024,1024]{1,0:T(8,128)(2,1)S(1)} %copy-done) | data formatting | bytes 4194304
Async XLA Ops:
  125.2 3.3 %copy-start = (bf16[1024,1024]{1,0:T(8,128)(2,1)S(1)}, bf16[1024,1024]{1,0:T(8,128)(2,1)}, u32[]{:S(2)}) copy-start(bf16[1024,1024]{1,0:T(8,128)(2,1)} %get-tuple-element.5) | copy-start | bytes 6291460

commit v5 on v4

--- a/solution.py
+++ b/solution.py
@@ -83,7 +83,8 @@
 
     def each_send(act):
         for part in range(2):
-            for block in range(total):
+            for turn in sorted(range(total), key=lambda d: (d == 0, abs(2 * d - total), d)):
+                block = lax.rem(home + turn, total)
                 target = stride * block + lane
 
                 @pl.when(me != target)

time: 130 us -> 130 us (level)
  no operation moved by 1% of the time
where the time goes in v5:
time: 130 us
  Pallas kernels  124 us (95%)
  local copies, waits for them, and re-layouts  4.63 us (4%)
    pallas_call x1, Pallas kernels, body(): pl.pallas_call(functools.partial(kernel, n, total), out_shape=(jax.ShapeD...  124 us
    unnamed x4, local copies, waits for them, and re-layouts  4.63 us

profile of v5, /device:TPU:2, one launch (start us, length us, event | category | flops | bytes accessed | tf_op | source)
XLA Modules:
  0.0 129.8 jit_solution(12965139943554516972)
XLA Ops:
  0.6 124.5 %shard_map.50 = (bf16[2,256,2048]{2,1,0:T(8,128)(2,1)}, bf16[1024,1024]{1,0:T(8,128)(2,1)}) custom-call(s32[8]{0:T(128)} %count_ref.1, s32[2,8]{1,0:T(2,128)} %owner_ref.1, bf16[2,256,2048]{2,1,0:T(8,128)(2,1)} %g_ref.1), custom_call_target="tpu_custom_call" | custom-call | tf_op jit(solution)/shard_map/pallas_call | solution.py:314
  125.1 0.0 copy-start
  125.1 3.3 %copy.7 = bf16[2,256,2048]{2,1,0:T(8,128)(2,1)} copy(bf16[2,256,2048]{2,1,0:T(8,128)(2,1)} %get-tuple-element.4) | data formatting | bytes 4194304
  128.5 0.0 copy-done
  128.5 1.3 %copy.8 = bf16[1024,1024]{1,0:T(8,128)(2,1)} copy(bf16[1024,1024]{1,0:T(8,128)(2,1)S(1)} %copy-done) | data formatting | bytes 4194304
Async XLA Ops:
  125.1 3.3 %copy-start = (bf16[1024,1024]{1,0:T(8,128)(2,1)S(1)}, bf16[1024,1024]{1,0:T(8,128)(2,1)}, u32[]{:S(2)}) copy-start(bf16[1024,1024]{1,0:T(8,128)(2,1)} %get-tuple-element.5) | copy-start | bytes 6291460

commit v6 on v4

--- a/solution.py
+++ b/solution.py
@@ -82,15 +82,20 @@
             recv_sem=in_recv.at[part, source], device_id=to(target), device_id_type=MESH)
 
     def each_send(act):
-        for part in range(2):
-            for block in range(total):
-                target = stride * block + lane
-
-                @pl.when(me != target)
-                def _():
-                    act(row_copy(block, part, me, target))
-
-    each_send(lambda copy: copy.start())
+        for turn in sorted(range(total), key=lambda d: (min(d, total - d), d)):
+            block = lax.rem(home + turn, total)
+            target = stride * block + lane
+
+            @pl.when(me != target)
+            def _():
+                act(block, target)
+
+    def follow(block, target):
+        row_copy(block, 0, me, target).wait_send()
+        row_copy(block, 1, me, target).start()
+
+    each_send(lambda block, target: row_copy(block, 0, me, target).start())
+    each_send(follow)
 
     def strip_copy(k, s, target, send_sem):
         piece = roots.at[k, pl.ds(s * STRIP, STRIP), pl.ds(0, (s + 1) * STRIP)]
@@ -256,9 +261,9 @@
     def _(step):
         k = pick(home * total + step, [p for line in order for p in line])
 
-        @pl.when(jnp.logical_not(is_home & (k == home)))
-        def _():
-            for s in range(STRIPS):
+        for s in range(STRIPS):
+            @pl.when(jnp.logical_not(is_home & (k == home)))
+            def _():
                 strip_copy(k, s, me, up_send.at[k, s]).wait_recv()
 
                 @pl.when(is_home)
@@ -269,14 +274,10 @@
                 def _():
                     beside_pass(k, s, lambda copy: copy.start())
 
-        def mirror(row0, column0, size):
-            piece = roots[k, pl.ds(row0, size), pl.ds(column0, size)]
-            roots[k, pl.ds(column0, size), pl.ds(row0, size)] = piece.T
-
-        for i in range(TILES):
-            mirror(i * TILE + STRIP, i * TILE, STRIP)
-            for j in range(i):
-                mirror(i * TILE, j * TILE, TILE)
+            row0 = s * STRIP
+            if s > 0:
+                roots[k, :row0, row0:row0 + STRIP] = roots[k, row0:row0 + STRIP, :row0].T
+
         layer = k // per_device
         column = lax.rem(k, per_device)
         owner = owner_ref[layer, tp * per_device + column]
@@ -288,7 +289,7 @@
             update_ref[layer, :, out_at] = dot(masked[k], roots[k, :, at]).astype(jnp.bfloat16)
             owned_ref[at, :] = jnp.where(owner == me, roots[k, at, :], owned_ref[at, :])
 
-    each_send(lambda copy: copy.wait_send())
+    each_send(lambda block, target: row_copy(block, 1, me, target).wait_send())
 
     @pl.loop(0, total)
     def _(k):
@@ -310,6 +311,9 @@
     smem = pl.BlockSpec(memory_space=pltpu.SMEM)
     square = (BLOCK, BLOCK)
     dma = pltpu.SemaphoreType.DMA
+    row_bytes = 2 * row_slots * BLOCK
+    square_bytes = 2 * BLOCK * BLOCK
+    held = (n + 3 * total) * row_bytes + (total + 8) * square_bytes + TILE * BLOCK * 4
     return pl.pallas_call(
         functools.partial(kernel, n, total),
         out_shape=(
@@ -336,7 +340,7 @@
             dma((total, STRIPS)),
         ],
         compiler_params=pltpu.CompilerParams(
-            collective_id=0, has_side_effects=True, vmem_limit_bytes=56 * 2**20
+            collective_id=0, has_side_effects=True, vmem_limit_bytes=held + 6 * 2**20
         ),
     )(row_counts, block_owner, gradients)
 

time: 130 us -> 126 us (0.969)
  the two profiles are of different devices: /device:TPU:2 before, /device:TPU:0 now
where the time goes in v6:
time: 126 us; the launch traced here: 124 us
  Pallas kernels  118 us (94%)
  local copies, waits for them, and re-layouts  5.56 us (4%)
    pallas_call x1, Pallas kernels, body(): pl.pallas_call(functools.partial(kernel, n, total), out_shape=(jax.ShapeD...  118 us
    unnamed x8, local copies, waits for them, and re-layouts  5.56 us

profile of v6, /device:TPU:0, one launch (start us, length us, event | category | flops | bytes accessed | tf_op | source)
XLA Modules:
  0.0 124.5 jit_solution(4745018468092256874)
XLA Ops:
  0.6 0.0 copy-start
  0.6 1.6 %copy-done = bf16[2,256,2048]{2,1,0:T(8,128)(2,1)S(1)} copy-done((bf16[2,256,2048]{2,1,0:T(8,128)(2,1)S(1)}, bf16[2,256,2048]{2,1,0:T(8,128)(2,1)}, u32[]{:S(2)}) %copy-start) | copy-done | bytes 2097176
  2.2 0.0 copy-start.1
  2.2 0.7 copy-done.1
  2.9 0.0 copy-start.2
  2.9 0.7 copy-done.2
  3.6 118.2 %shard_map.50 = (bf16[2,256,2048]{2,1,0:T(8,128)(2,1)S(1)}, bf16[1024,1024]{1,0:T(8,128)(2,1)S(1)}) custom-call(s32[8]{0:T(128)S(1)} %copy-done.2, s32[2,8]{1,0:T(2,128)S(1)} %copy-done.1, bf16[2,256,2048]{2,1,0:T(8,128)(2,1)S(1)} %copy-done), custom_call_target="tpu_custom_call" | custom-call | tf_op jit(solution)/shard_map/pallas_call | solution.py:317
  121.8 1.3 %copy.7 = bf16[2,256,2048]{2,1,0:T(8,128)(2,1)} copy(bf16[2,256,2048]{2,1,0:T(8,128)(2,1)S(1)} %get-tuple-element.4) | data formatting | bytes 4194304
  123.1 1.3 %copy.8 = bf16[1024,1024]{1,0:T(8,128)(2,1)} copy(bf16[1024,1024]{1,0:T(8,128)(2,1)S(1)} %get-tuple-element.5) | data formatting | bytes 4194304
Async XLA Ops:
  0.6 1.6 %copy-start = (bf16[2,256,2048]{2,1,0:T(8,128)(2,1)S(1)}, bf16[2,256,2048]{2,1,0:T(8,128)(2,1)}, u32[]{:S(2)}) copy-start(bf16[2,256,2048]{2,1,0:T(8,128)(2,1)} %g_ref.1) | copy-start | bytes 6291460
  2.2 0.7 copy-start.1
  2.9 0.7 copy-start.2

commit v7 on v6

--- a/solution.py
+++ b/solution.py
@@ -10,11 +10,12 @@
 BLOCK = 1024
 damping = 0.01
 TILE = 256
-STRIP = 128
+STRIP = 64
 STRIPS = BLOCK // STRIP
 TILES = BLOCK // TILE
+LANES = 128
 CHUNK = 16
-DETOUR = (2, 6, 7)
+DETOUR = (4, 5, 12, 13, 14, 15)
 MESH = pl.DeviceIdType.MESH
 
 
@@ -98,7 +99,7 @@
     each_send(follow)
 
     def strip_copy(k, s, target, send_sem):
-        piece = roots.at[k, pl.ds(s * STRIP, STRIP), pl.ds(0, (s + 1) * STRIP)]
+        piece = roots.at[k, pl.ds(s * STRIP, STRIP), pl.ds(0, ((s + 1) * STRIP + LANES - 1) // LANES * LANES)]
         return pltpu.make_async_remote_copy(
             src_ref=piece, dst_ref=piece, send_sem=send_sem, recv_sem=root_recv.at[k, s],
             device_id=to(target), device_id_type=MESH)
@@ -274,9 +275,9 @@
                 def _():
                     beside_pass(k, s, lambda copy: copy.start())
 
-            row0 = s * STRIP
-            if s > 0:
-                roots[k, :row0, row0:row0 + STRIP] = roots[k, row0:row0 + STRIP, :row0].T
+            row0 = (s + 1) * STRIP - LANES
+            if row0 > 0 and row0 % LANES == 0:
+                roots[k, :row0, row0:row0 + LANES] = roots[k, row0:row0 + LANES, :row0].T
 
         layer = k // per_device
         column = lax.rem(k, per_device)

time: 126 us -> 127 us (level)
  Pallas kernels: 118 us -> 120 us
where the time goes in v7:
time: 127 us; the launch traced here: 126 us
  Pallas kernels  120 us (94%)
  local copies, waits for them, and re-layouts  5.56 us (4%)
    pallas_call x1, Pallas kernels, body(): pl.pallas_call(functools.partial(kernel, n, total), out_shape=(jax.ShapeD...  120 us
    unnamed x8, local copies, waits for them, and re-layouts  5.56 us

profile of v7, /device:TPU:0, one launch (start us, length us, event | category | flops | bytes accessed | tf_op | source)
XLA Modules:
  0.0 125.7 jit_solution(11326715074715611615)
XLA Ops:
  0.6 0.0 copy-start
  0.6 1.6 %copy-done = bf16[2,256,2048]{2,1,0:T(8,128)(2,1)S(1)} copy-done((bf16[2,256,2048]{2,1,0:T(8,128)(2,1)S(1)}, bf16[2,256,2048]{2,1,0:T(8,128)(2,1)}, u32[]{:S(2)}) %copy-start) | copy-done | bytes 2097176
  2.2 0.0 copy-start.1
  2.2 0.7 copy-done.1
  2.9 0.0 copy-start.2
  2.9 0.7 copy-done.2
  3.6 119.5 %shard_map.50 = (bf16[2,256,2048]{2,1,0:T(8,128)(2,1)S(1)}, bf16[1024,1024]{1,0:T(8,128)(2,1)S(1)}) custom-call(s32[8]{0:T(128)S(1)} %copy-done.2, s32[2,8]{1,0:T(2,128)S(1)} %copy-done.1, bf16[2,256,2048]{2,1,0:T(8,128)(2,1)S(1)} %copy-done), custom_call_target="tpu_custom_call" | custom-call | tf_op jit(solution)/shard_map/pallas_call | solution.py:318
  123.1 1.3 %copy.7 = bf16[2,256,2048]{2,1,0:T(8,128)(2,1)} copy(bf16[2,256,2048]{2,1,0:T(8,128)(2,1)S(1)} %get-tuple-element.4) | data formatting | bytes 4194304
  124.4 1.3 %copy.8 = bf16[1024,1024]{1,0:T(8,128)(2,1)} copy(bf16[1024,1024]{1,0:T(8,128)(2,1)S(1)} %get-tuple-element.5) | data formatting | bytes 4194304
Async XLA Ops:
  0.6 1.6 %copy-start = (bf16[2,256,2048]{2,1,0:T(8,128)(2,1)S(1)}, bf16[2,256,2048]{2,1,0:T(8,128)(2,1)}, u32[]{:S(2)}) copy-start(bf16[2,256,2048]{2,1,0:T(8,128)(2,1)} %g_ref.1) | copy-start | bytes 6291460
  2.2 0.7 copy-start.1
  2.9 0.7 copy-start.2

commit v8 on v6

--- a/solution.py
+++ b/solution.py
@@ -257,9 +257,12 @@
 
     owned_ref[...] = jnp.zeros_like(owned_ref)
 
+    def kth(step):
+        return pick(home * total + step, [p for line in order for p in line])
+
     @pl.loop(0, total)
     def _(step):
-        k = pick(home * total + step, [p for line in order for p in line])
+        k = kth(step)
 
         for s in range(STRIPS):
             @pl.when(jnp.logical_not(is_home & (k == home)))
@@ -278,16 +281,19 @@
             if s > 0:
                 roots[k, :row0, row0:row0 + STRIP] = roots[k, row0:row0 + STRIP, :row0].T
 
-        layer = k // per_device
-        column = lax.rem(k, per_device)
-        owner = owner_ref[layer, tp * per_device + column]
-
-        @pl.loop(0, TILES)
-        def _(i):
-            at = pl.ds(pl.multiple_of(i * TILE, TILE), TILE)
-            out_at = pl.ds(pl.multiple_of(column * BLOCK + i * TILE, TILE), TILE)
-            update_ref[layer, :, out_at] = dot(masked[k], roots[k, :, at]).astype(jnp.bfloat16)
-            owned_ref[at, :] = jnp.where(owner == me, roots[k, at, :], owned_ref[at, :])
+        @pl.loop(jnp.where(step == 1, 0, step), jnp.where(step == 0, 0, step + 1))
+        def _(done):
+            k = kth(done)
+            layer = k // per_device
+            column = lax.rem(k, per_device)
+            owner = owner_ref[layer, tp * per_device + column]
+
+            @pl.loop(0, TILES)
+            def _(i):
+                at = pl.ds(pl.multiple_of(i * TILE, TILE), TILE)
+                out_at = pl.ds(pl.multiple_of(column * BLOCK + i * TILE, TILE), TILE)
+                update_ref[layer, :, out_at] = dot(masked[k], roots[k, :, at]).astype(jnp.bfloat16)
+                owned_ref[at, :] = jnp.where(owner == me, roots[k, at, :], owned_ref[at, :])
 
     each_send(lambda block, target: row_copy(block, 1, me, target).wait_send())
 

time: 126 us -> 128 us (1.016); the launches traced: 124 us -> 128 us
  Pallas kernels: 118 us -> 122 us
    pallas_call x1, Pallas kernels: 118 us -> 122 us  [body(): pl.pallas_call(functools.partial(kernel, n, total), out_shape=(jax.ShapeD...]
where the time goes in v8:
time: 128 us
  Pallas kernels  122 us (95%)
  local copies, waits for them, and re-layouts  5.56 us (4%)
    pallas_call x1, Pallas kernels, body(): pl.pallas_call(functools.partial(kernel, n, total), out_shape=(jax.ShapeD...  122 us
    unnamed x8, local copies, waits for them, and re-layouts  5.56 us

profile of v8, /device:TPU:0, one launch (start us, length us, event | category | flops | bytes accessed | tf_op | source)
XLA Modules:
  0.0 128.0 jit_solution(1643212275820911063)
XLA Ops:
  0.6 0.0 copy-start
  0.6 1.6 %copy-done = bf16[2,256,2048]{2,1,0:T(8,128)(2,1)S(1)} copy-done((bf16[2,256,2048]{2,1,0:T(8,128)(2,1)S(1)}, bf16[2,256,2048]{2,1,0:T(8,128)(2,1)}, u32[]{:S(2)}) %copy-start) | copy-done | bytes 2097176
  2.2 0.0 copy-start.1
  2.2 0.7 copy-done.1
  2.9 0.0 copy-start.2
  2.9 0.7 copy-done.2
  3.6 121.8 %shard_map.50 = (bf16[2,256,2048]{2,1,0:T(8,128)(2,1)S(1)}, bf16[1024,1024]{1,0:T(8,128)(2,1)S(1)}) custom-call(s32[8]{0:T(128)S(1)} %copy-done.2, s32[2,8]{1,0:T(2,128)S(1)} %copy-done.1, bf16[2,256,2048]{2,1,0:T(8,128)(2,1)S(1)} %copy-done), custom_call_target="tpu_custom_call" | custom-call | tf_op jit(solution)/shard_map/pallas_call | solution.py:323
  125.4 1.3 %copy.7 = bf16[2,256,2048]{2,1,0:T(8,128)(2,1)} copy(bf16[2,256,2048]{2,1,0:T(8,128)(2,1)S(1)} %get-tuple-element.4) | data formatting | bytes 4194304
  126.7 1.3 %copy.8 = bf16[1024,1024]{1,0:T(8,128)(2,1)} copy(bf16[1024,1024]{1,0:T(8,128)(2,1)S(1)} %get-tuple-element.5) | data formatting | bytes 4194304
Async XLA Ops:
  0.6 1.6 %copy-start = (bf16[2,256,2048]{2,1,0:T(8,128)(2,1)S(1)}, bf16[2,256,2048]{2,1,0:T(8,128)(2,1)}, u32[]{:S(2)}) copy-start(bf16[2,256,2048]{2,1,0:T(8,128)(2,1)} %g_ref.1) | copy-start | bytes 6291460
  2.2 0.7 copy-start.1
  2.9 0.7 copy-start.2
